TPU v7x, 32 devices: a whole 2x2x4 slice. The times are simulated.
32 devices in a mesh: chan: 8 (over z, y), tm: 4 (over x, core).
Axes of the slice: x: 2, y: 2, z: 4, core: 2. Of those that a mesh axis runs over, the one named last changes fastest.
Arguments:
- recording: bfloat16 [4096, 8192], P('chan', 'tm'), may hold values from -6 to 6
- band_taps: bfloat16 [3, 255], replicated, may hold values from -0.375 to 0.375
- channel_gain: float32 [4096], P('chan'), may hold values from 0.25 to 2
- range_test: bfloat16 [8192, 64], P('tm'), may hold values from -0.0625 to 0.0625
- corange_test: bfloat16 [64, 4096], P(None, 'chan'), may hold values from -0.09375 to 0.09375
- core_left: bfloat16 [128, 4096], P(None, 'chan'), may hold values from -0.09375 to 0.09375
- core_right: bfloat16 [8192, 128], P('tm'), may hold values from -0.0625 to 0.0625
Outputs:
- strain_rate: bfloat16 [3, 4096, 8192], P(None, 'chan', 'tm')
- range_sketch: float32 [3, 4096, 64], P(None, 'chan')
- corange_sketch: float32 [3, 64, 8192], P(None, None, 'tm')
- core_sketch: float32 [3, 128, 128], replicated
All inputs are finite; a program needn't handle non-finite values.
Results may differ from a plain program's by a relative error of at most 0.0052.
Values may be sent and summed in bfloat16 or wider, within the bound.
A program may use at most 64 MiB of HBM per device.

v0:
```python
import jax
import jax.numpy as jnp
from jax import lax
from jax.sharding import PartitionSpec as P


def padded_2(block, sides, width):
    for axis, dim in sides:
        count = lax.axis_size(axis)
        forward = [(i, i + 1) for i in range(count - 1)]
        backward = [(target, source) for source, target in forward]
        low = lax.ppermute(
            lax.slice_in_dim(block, block.shape[dim] - width, None, axis=dim), axis, forward
        )
        high = lax.ppermute(lax.slice_in_dim(block, 0, width, axis=dim), axis, backward)
        block = jnp.concatenate([low, block, high], axis=dim)
    return block


def on_device(recording, band_taps, channel_gain, range_test, corange_test, core_left, core_right):
    tap_count = band_taps.shape[1]
    half_width = tap_count // 2
    channels, samples = recording.shape
    padded = padded_2(recording, (("tm", 1),), half_width)
    padded = jnp.pad(padded, ((0, 0), (0, 256 - 2 * half_width)))
    blocks = samples // 128
    lead_block = padded[:, :samples].reshape(channels, blocks, 128)
    mid_block = padded[:, 128 : samples + 128].reshape(channels, blocks, 128)
    tail_block = padded[:, 256 : samples + 256].reshape(channels, blocks, 128)
    windows = jnp.concatenate([lead_block, mid_block, tail_block], axis=2)
    window_pos = lax.broadcasted_iota(jnp.int32, (384, 128), 0)
    output_pos = lax.broadcasted_iota(jnp.int32, (384, 128), 1)
    offset = window_pos - output_pos
    inside = (offset >= 0) & (offset < tap_count)
    picked = jnp.take(band_taps, jnp.clip(offset, 0, tap_count - 1), axis=1)
    toeplitz = jnp.where(inside[None], picked, jnp.zeros_like(picked))
    band_count = band_taps.shape[0]
    filtered = jnp.einsum("cnw,bwo->bcno", windows, toeplitz, preferred_element_type=jnp.float32)
    filtered = filtered.reshape(band_count, channels, samples).astype(jnp.bfloat16)
    rimmed = padded_2(filtered, (("chan", 1),), 1)
    difference = rimmed[:, 2:].astype(jnp.float32) - rimmed[:, :-2].astype(jnp.float32)
    strain_rate = (channel_gain[None, :, None] * difference).astype(jnp.bfloat16)
    range_part = jnp.einsum(
        "bct,tk->bck", strain_rate, range_test, preferred_element_type=jnp.float32
    )
    corange_part = jnp.einsum(
        "lc,bct->blt", corange_test, strain_rate, preferred_element_type=jnp.float32
    )
    high = lax.Precision.HIGHEST
    projected = jnp.einsum(
        "bct,ts->bcs", strain_rate, core_right, preferred_element_type=jnp.float32
    )
    range_sketch, projected_sum = lax.psum((range_part, projected), "tm")
    corange_sketch = lax.psum(corange_part, "chan")
    core_term = jnp.einsum(
        "rc,bcs->brs", core_left.astype(jnp.float32), projected_sum, precision=high
    )
    core_sketch = lax.psum(core_term, "chan")
    return (strain_rate, range_sketch, corange_sketch, core_sketch)


def solution(mesh):
    in_specs = (
        P("chan", "tm"),
        P(),
        P("chan"),
        P("tm", None),
        P(None, "chan"),
        P(None, "chan"),
        P("tm", None),
    )
    out_specs = (P(None, "chan", "tm"), P(None, "chan", None), P(None, None, "tm"), P())
    return jax.shard_map(
        on_device, mesh=mesh, in_specs=in_specs, out_specs=out_specs, check_vma=False
    )
```

profile of v0, /device:TPU:0, one launch (start us, length us, event | category | flops | bytes accessed | tf_op | source)
XLA Modules:
  0.0 424.9 jit_solution(13206108507670665187)
XLA Ops:
  7.2 0.0 copy-start
  7.2 0.0 all-reduce.8.cloned.1.call-start
  7.2 2.9 copy.20
  10.1 0.7 fusion.31
  10.9 2.4 collective-permute-start
  13.2 1.3 collective-permute-start.1
  14.5 0.1 fusion.16
  14.6 0.8 copy.18
  15.4 170.7 %gather_fusion = bf16[49152,3]{1,0:T(8,128)(2,1)} fusion(bf16[3,255]{0,1:T(8,128)(2,1)S(1)} %copy.18, s32[49152]{0:T(1024)S(1)} %fusion.16), kind=kCustom, calls=%fused_computation | custom fusion | bytes 786432 | tf_op jit(solution)/shard_map/jit(_take)/gather | solution.py:35
  186.2 16.1 %copy.19 = bf16[384,128,3]{0,1,2:T(8,128)(2,1)S(1)} copy(bf16[384,128,3]{2,1,0:T(8,128)(2,1)} %bitcast.43) | data formatting | bytes 589824 | tf_op jit(solution)/shard_map/jit(_take)/gather | solution.py:35
  202.3 0.1 fusion.21
  202.4 0.0 collective-permute-done
  202.4 0.0 collective-permute-done.1
  202.4 11.3 %concatenate.21 = bf16[512,2302]{0,1:T(8,128)(2,1)} concatenate(bf16[512,127]{0,1:T(8,128)(2,1)S(1)} %collective-permute-done, bf16[512,2048]{0,1:T(8,128)(2,1)S(1)} %copy.20, bf16[512,127]{0,1:T(8,128)(2,1)S(1)} %collective-permute-done.1), dimensions={1} | concatenate | bytes 4714496 | tf_op jit(solution)/shard_map/concatenate | solution.py:16
  213.7 3.1 pad_slice_fusion
  216.8 3.9 copy.27
  220.7 2.5 pad_maximum_fusion.3
  223.2 4.1 copy.26
  227.3 3.9 copy.25
  231.2 0.0 copy-done.2
  231.2 6.9 %fusion.5 = bf16[3,128,512,16]{2,1,3,0:T(8,128)(2,1)} fusion(bf16[512,16,128]{2,0,1:T(8,128)(2,1)S(1)} %copy-done.2, bf16[512,16,128]{2,0,1:T(8,128)(2,1)} %copy.26, bf16[512,16,128]{2,0,1:T(8,128)(2,1)} %copy.25, bf16[384,128,3]{0,1,2:T(8,128)(2,1)S(1)} %copy.19, pred[384,128]{0,1:T(8,128)(4,1)S(1)} %get-tuple-element.23, ...), kind=kOutput, calls=%fused_computation.10 | convolution fusion | flops 2438234112 | bytes 12976128 | tf_op jit(solution)/shard_map/cnw,bwo->bcno/dot_general | solution.py:38
  238.1 8.9 %copy.29 = bf16[3,512,2048]{2,1,0:T(8,128)(2,1)} copy(bf16[3,512,2048]{1,2,0:T(8,128)(2,1)} %bitcast.47) | data formatting | bytes 12582912 | tf_op jit(solution)/shard_map/convert_element_type | solution.py:39
  247.0 1.0 fusion.30
  248.0 4.3 %collective-permute-start.3 = (bf16[3,1,2048]{2,1,0:T(2,128)(2,1)S(1)}, bf16[3,1,2048]{2,1,0:T(2,128)(2,1)S(1)}, u32[]{:S(2)}, u32[]{:S(2)}) collective-permute-start(bf16[3,1,2048]{2,1,0:T(2,128)(2,1)S(1)} %get-tuple-element.17), channel_id=1, source_target_pairs={{0,4},{4,8},{8,12},{12,16},{16,20},{20,24},{24,28},{1,5},{5,9},{9,... | collective-permute-start | bytes 36872 | tf_op jit(solution)/shard_map/ppermute | solution.py:12
  252.3 0.0 copy-start.3
  252.3 1.4 collective-permute-start.2
  253.7 0.1 collective-permute-done.3
  253.8 4.4 %collective-permute-done.2 = bf16[3,1,2048]{2,1,0:T(2,128)(2,1)S(1)} collective-permute-done((bf16[3,1,2048]{2,1,0:T(2,128)(2,1)S(1)}, bf16[3,1,2048]{2,1,0:T(2,128)(2,1)S(1)}, u32[]{:S(2)}, u32[]{:S(2)}) %collective-permute-start.2) | collective-permute-done | bytes 12320 | tf_op jit(solution)/shard_map/ppermute | solution.py:15
  258.2 0.0 copy-done.6
  258.2 8.3 %multiply_convert_fusion = bf16[3,512,2048]{2,1,0:T(8,128)(2,1)S(1)} fusion(bf16[3,512,2048]{2,1,0:T(8,128)(2,1)} %copy.29, bf16[3,1,2048]{2,1,0:T(2,128)(2,1)S(1)} %collective-permute-done.3, bf16[3,1,2048]{2,1,0:T(2,128)(2,1)S(1)} %collective-permute-done.2, f32[512]{0:T(512)S(1)} %copy-done.6), kind=kLoop, calls=%fused_computation.1 | loop fusion | flops 34603008 | bytes 12609536 | tf_op jit(solution)/shard_map/convert_element_type | solution.py:42
  266.4 0.0 copy-done.3
  266.4 0.0 copy-start.1
  266.4 0.0 copy-start.5
  266.5 2.8 fusion.13
  269.3 0.0 copy-done.1
  269.3 0.0 copy-done
  269.3 3.1 fusion.6
  272.4 0.0 all-reduce.8.cloned.1.call-update
  272.4 0.0 all-reduce.6.cloned.1.call-start
  272.5 0.0 copy-done.5
  272.5 5.1 %convolution_bitcast_fusion = f32[3,64,2048]{2,1,0:T(8,128)} fusion(bf16[3,512,2048]{2,1,0:T(8,128)(2,1)} %copy-done.1, bf16[64,512]{1,0:T(8,128)(2,1)S(1)} %copy-done.5), kind=kOutput, calls=%fused_computation.11 | convolution fusion | flops 402653184 | bytes 7929856 | tf_op jit(solution)/shard_map/lc,bct->blt/dot_general | solution.py:46
  277.6 36.1 %all-reduce.8.cloned.1.call-done = (f32[3,512,64]{1,2,0:T(8,128)}, f32[3,512,128]{1,2,0:T(8,128)}) async-done(((f32[3,512,64]{1,2,0:T(8,128)}, f32[3,512,128]{1,2,0:T(8,128)}), (f32[3,512,64]{1,2,0:T(8,128)}, f32[3,512,128]{1,2,0:T(8,128)})) %all-reduce.8.cloned.1.call-update) | async-done | bytes 1179664 | tf_op jit(solution)/shard_map/psum | solution.py:53
  313.7 2.3 convolution_bitcast_fusion.1
  316.0 0.0 all-reduce.6.cloned.1.call-update
  316.0 95.8 %all-reduce.6.cloned.1.call-done = (f32[3,64,2048]{2,1,0:T(8,128)}, f32[3,128,128]{1,2,0:T(8,128)}) async-done(((f32[3,64,2048]{2,1,0:T(8,128)}, f32[3,128,128]{1,2,0:T(8,128)}), (f32[3,64,2048]{2,1,0:T(8,128)}, f32[3,128,128]{1,2,0:T(8,128)})) %all-reduce.6.cloned.1.call-update) | async-done | bytes 1769488 | tf_op jit(solution)/shard_map/psum | solution.py:54
  411.8 1.7 copy.32
  413.6 1.8 copy.38
  415.3 2.7 copy.39
  (4 shorter events, 0.0 us)
Async XLA Ops:
  7.2 262.1 %copy-start = (bf16[2048,128]{1,0:T(8,128)(2,1)S(1)}, bf16[2048,128]{1,0:T(8,128)(2,1)}, u32[]{:S(2)}) copy-start(bf16[2048,128]{1,0:T(8,128)(2,1)} %param.13) | copy-start | bytes 1572868
  7.2 306.5 %all-reduce.8.cloned.1.call-start = ((), (), s32[]{:S(2)}) async-start(), calls=%async_computation.1 | async-start | bytes 2359296 | tf_op jit(solution)/shard_map/psum | solution.py:53
  10.9 191.5 %collective-permute-start = (bf16[512,127]{0,1:T(8,128)(2,1)}, bf16[512,127]{0,1:T(8,128)(2,1)S(1)}, u32[]{:S(2)}, u32[]{:S(2)}) collective-permute-start(bf16[512,127]{0,1:T(8,128)(2,1)} %get-tuple-element.21), channel_id=1, source_target_pairs={{0,1},{1,2},{2,3},{4,5},{5,6},{6,7},{8,9},{9,10},{10,11},{12,13},{... | collective-permute-start | bytes 390152 | tf_op jit(solution)/shard_map/ppermute | solution.py:12
  13.2 189.1 %collective-permute-start.1 = (bf16[512,127]{0,1:T(8,128)(2,1)}, bf16[512,127]{0,1:T(8,128)(2,1)S(1)}, u32[]{:S(2)}, u32[]{:S(2)}) collective-permute-start(bf16[512,127]{0,1:T(8,128)(2,1)} %get-tuple-element.20), channel_id=1, source_target_pairs={{1,0},{2,1},{3,2},{5,4},{6,5},{7,6},{9,8},{10,9},{11,10},{13,12},{... | collective-permute-start | bytes 390152 | tf_op jit(solution)/shard_map/ppermute | solution.py:15
  223.2 8.0 %copy-start.2 = (bf16[512,16,128]{2,0,1:T(8,128)(2,1)S(1)}, bf16[512,16,128]{2,0,1:T(8,128)(2,1)}, u32[]{:S(2)}) copy-start(bf16[512,16,128]{2,0,1:T(8,128)(2,1)} %copy.27) | copy-start | bytes 6291460
  238.1 20.1 %copy-start.6 = (f32[512]{0:T(512)S(1)}, f32[512]{0:T(512)}, u32[]{:S(2)}) copy-start(f32[512]{0:T(512)} %param.9) | copy-start | bytes 6148
  248.0 5.8 %collective-permute-start.3 = (bf16[3,1,2048]{2,1,0:T(2,128)(2,1)S(1)}, bf16[3,1,2048]{2,1,0:T(2,128)(2,1)S(1)}, u32[]{:S(2)}, u32[]{:S(2)}) collective-permute-start(bf16[3,1,2048]{2,1,0:T(2,128)(2,1)S(1)} %get-tuple-element.17), channel_id=1, source_target_pairs={{0,4},{4,8},{8,12},{12,16},{16,20},{20,24},{24,28},{1,5},{5,9},{9,... | collective-permute-start | bytes 36872 | tf_op jit(solution)/shard_map/ppermute | solution.py:12
  252.3 14.1 %copy-start.3 = (bf16[2048,64]{0,1:T(8,128)(2,1)S(1)}, bf16[2048,64]{0,1:T(8,128)(2,1)}, u32[]{:S(2)}) copy-start(bf16[2048,64]{0,1:T(8,128)(2,1)} %param.10) | copy-start | bytes 786436
  252.3 5.9 %collective-permute-start.2 = (bf16[3,1,2048]{2,1,0:T(2,128)(2,1)S(1)}, bf16[3,1,2048]{2,1,0:T(2,128)(2,1)S(1)}, u32[]{:S(2)}, u32[]{:S(2)}) collective-permute-start(bf16[3,1,2048]{2,1,0:T(2,128)(2,1)S(1)} %get-tuple-element.16), channel_id=1, source_target_pairs={{4,0},{8,4},{12,8},{16,12},{20,16},{24,20},{28,24},{5,1},{9,5},{13... | collective-permute-start | bytes 36872 | tf_op jit(solution)/shard_map/ppermute | solution.py:15
  266.4 2.8 copy-start.1
  266.4 6.0 %copy-start.5 = (bf16[64,512]{1,0:T(8,128)(2,1)S(1)}, bf16[64,512]{1,0:T(8,128)(2,1)}, u32[]{:S(2)}) copy-start(bf16[64,512]{1,0:T(8,128)(2,1)} %param.11) | copy-start | bytes 196612
  272.4 41.3 %copy-start.4 = (bf16[128,512]{1,0:T(8,128)(2,1)S(1)}, bf16[128,512]{1,0:T(8,128)(2,1)}, u32[]{:S(2)}) copy-start(bf16[128,512]{1,0:T(8,128)(2,1)} %param.12) | copy-start | bytes 393220
  272.4 139.4 %all-reduce.6.cloned.1.call-start = ((), (), s32[]{:S(2)}) async-start(), calls=%async_computation | async-start | bytes 3538944 | tf_op jit(solution)/shard_map/psum | solution.py:54
Sparse Core Ops, SparseCore 0:
  272.5 41.1 all-reduce.7
  317.9 93.9 all-reduce.5
where the time goes:
time: 427 us; the launch traced here: 425 us
  local copies, waits for them, and re-layouts  234 us (55%)
  waiting for transfers between devices  136 us (32%)
  matrix products  20.3 us (5%)
  between operations  14.2 us (3%)
  other arithmetic  10.9 us (3%)
  starting transfers between devices  9.4 us (2%)
    gather x2, local copies, waits for them, and re-layouts, on_device(): picked = jnp.take(band_taps, jnp.clip(offset, 0, tap_count - 1), axis=1)  187 us
    psum x1, waiting for transfers between devices, on_device(): corange_sketch = lax.psum(corange_part, 'chan')  95.8 us
    psum x1, waiting for transfers between devices, on_device(): range_sketch, projected_sum = lax.psum((range_part, projected), 'tm')  36.1 us
    concatenate x1, local copies, waits for them, and re-layouts, padded_2(): block = jnp.concatenate([low, block, high], axis=dim)  11.3 us
    unnamed x19, local copies, waits for them, and re-layouts  9.98 us
    convert_element_type x1, local copies, waits for them, and re-layouts, on_device(): filtered.reshape(band_count, channels, samples).astype(jnp.bfloat16)  8.93 us
  transfers between devices with their start and end apart: 6, of which 4 were waited for; matrix products, arithmetic and copies ran while one was open for 45% of the time, Pallas kernels for 0%

commit v1 on v0

--- a/solution.py
+++ b/solution.py
@@ -51,7 +51,11 @@
         "bct,ts->bcs", strain_rate, core_right, preferred_element_type=jnp.float32
     )
     range_sketch, projected_sum = lax.psum((range_part, projected), "tm")
-    corange_sketch = lax.psum(corange_part, "chan")
+    corange_sketch = corange_part
+    for hop in (1, 2, 4):
+        corange_sketch = corange_sketch + lax.ppermute(
+            corange_sketch, "chan", [(dev, dev ^ hop) for dev in range(8)]
+        )
     core_term = jnp.einsum(
         "rc,bcs->brs", core_left.astype(jnp.float32), projected_sum, precision=high
     )

time: 427 us -> 483 us (1.13)
  waiting for transfers between devices: 136 us -> 190 us
  starting transfers between devices: 9.4 us -> 16.2 us
    ppermute x0 -> x3, waiting for transfers between devices: none -> 69.8 us  [on_device(): lax.ppermute(corange_sketch, 'chan', [(dev, dev ^ hop) for dev in range(8)])]
    psum x1, waiting for transfers between devices: 95.8 us -> 79.5 us  [on_device(): core_sketch = lax.psum(core_term, 'chan')]
    ppermute x0 -> x3, starting transfers between devices: none -> 6.78 us  [on_device(): lax.ppermute(corange_sketch, 'chan', [(dev, dev ^ hop) for dev in range(8)])]
    unnamed x19 -> x20, local copies, waits for them, and re-layouts: 9.98 us -> 6.26 us
  transfers between devices with their start and end apart: 6 -> 9, of which waited for: 4 -> 6; matrix products, arithmetic and copies ran while one was open for 45% -> 41% of each run, Pallas kernels for 0% -> 0%
where the time goes in v1:
time: 483 us; the launch traced here: 481 us
  local copies, waits for them, and re-layouts  230 us (48%)
  waiting for transfers between devices  190 us (39%)
  matrix products  16.4 us (3%)
  starting transfers between devices  16.2 us (3%)
  between operations  14.2 us (3%)
  other arithmetic  14.1 us (3%)
    gather x2, local copies, waits for them, and re-layouts, on_device(): picked = jnp.take(band_taps, jnp.clip(offset, 0, tap_count - 1), axis=1)  187 us
    psum x1, waiting for transfers between devices, on_device(): core_sketch = lax.psum(core_term, 'chan')  79.5 us
    ppermute x3, waiting for transfers between devices, on_device(): lax.ppermute(corange_sketch, 'chan', [(dev, dev ^ hop) for dev in range(8)])  69.8 us
    psum x1, waiting for transfers between devices, on_device(): range_sketch, projected_sum = lax.psum((range_part, projected), 'tm')  36.4 us
    concatenate x1, local copies, waits for them, and re-layouts, padded_2(): block = jnp.concatenate([low, block, high], axis=dim)  11.3 us
  transfers between devices with their start and end apart: 9, of which 6 were waited for; matrix products, arithmetic and copies ran while one was open for 41% of the time, Pallas kernels for 0%

profile of v1, /device:TPU:0, one launch (start us, length us, event | category | flops | bytes accessed | tf_op | source)
XLA Modules:
  0.0 481.0 jit_solution(14583345309252918488)
XLA Ops:
  7.2 0.0 copy-start
  7.2 0.0 all-reduce.7.cloned.1.call-start
  7.2 2.9 copy.20
  10.1 0.7 fusion.31
  10.9 2.4 collective-permute-start
  13.2 1.3 collective-permute-start.1
  14.5 0.1 fusion.16
  14.6 0.8 copy.18
  15.4 170.7 %gather_fusion = bf16[49152,3]{1,0:T(8,128)(2,1)} fusion(bf16[3,255]{0,1:T(8,128)(2,1)S(1)} %copy.18, s32[49152]{0:T(1024)S(1)} %fusion.16), kind=kCustom, calls=%fused_computation | custom fusion | bytes 786432 | tf_op jit(solution)/shard_map/jit(_take)/gather | solution.py:35
  186.1 16.1 %copy.19 = bf16[384,128,3]{0,1,2:T(8,128)(2,1)S(1)} copy(bf16[384,128,3]{2,1,0:T(8,128)(2,1)} %bitcast.43) | data formatting | bytes 589824 | tf_op jit(solution)/shard_map/jit(_take)/gather | solution.py:35
  202.2 0.1 fusion.21
  202.3 11.3 %concatenate.21 = bf16[512,2302]{0,1:T(8,128)(2,1)} concatenate(bf16[512,127]{0,1:T(8,128)(2,1)S(1)} %collective-permute-done, bf16[512,2048]{0,1:T(8,128)(2,1)S(1)} %copy.20, bf16[512,127]{0,1:T(8,128)(2,1)S(1)} %collective-permute-done.1), dimensions={1} | concatenate | bytes 4714496 | tf_op jit(solution)/shard_map/concatenate | solution.py:16
  213.6 3.1 pad_slice_fusion
  216.7 3.9 copy.27
  220.6 2.5 pad_maximum_fusion.3
  223.1 4.0 copy.26
  227.2 3.9 copy.25
  231.1 6.9 %fusion.5 = bf16[3,128,512,16]{2,1,3,0:T(8,128)(2,1)} fusion(bf16[512,16,128]{2,0,1:T(8,128)(2,1)S(1)} %copy-done.2, bf16[512,16,128]{2,0,1:T(8,128)(2,1)} %copy.26, bf16[512,16,128]{2,0,1:T(8,128)(2,1)} %copy.25, bf16[384,128,3]{0,1,2:T(8,128)(2,1)S(1)} %copy.19, pred[384,128]{0,1:T(8,128)(4,1)S(1)} %get-tuple-element.21, ...), kind=kOutput, calls=%fused_computation.10 | convolution fusion | flops 2438234112 | bytes 12976128 | tf_op jit(solution)/shard_map/cnw,bwo->bcno/dot_general | solution.py:38
  238.0 8.9 %copy.29 = bf16[3,512,2048]{2,1,0:T(8,128)(2,1)} copy(bf16[3,512,2048]{1,2,0:T(8,128)(2,1)} %bitcast.47) | data formatting | bytes 12582912 | tf_op jit(solution)/shard_map/convert_element_type | solution.py:39
  246.9 1.0 fusion.30
  247.9 4.3 collective-permute-start.3
  252.2 0.0 copy-start.6
  252.2 1.4 collective-permute-start.2
  253.6 0.1 collective-permute-done.3
  253.7 4.4 collective-permute-done.2
  258.1 8.3 %multiply_convert_fusion = bf16[3,512,2048]{2,1,0:T(8,128)(2,1)S(1)} fusion(bf16[3,512,2048]{2,1,0:T(8,128)(2,1)} %copy.29, bf16[3,1,2048]{2,1,0:T(2,128)(2,1)S(1)} %collective-permute-done.3, bf16[3,1,2048]{2,1,0:T(2,128)(2,1)S(1)} %collective-permute-done.2, f32[512]{0:T(512)S(1)} %copy-done.7), kind=kLoop, calls=%fused_computation.1 | loop fusion | flops 34603008 | bytes 12609536 | tf_op jit(solution)/shard_map/convert_element_type | solution.py:42
  266.3 0.0 copy-start.1
  266.3 1.3 convolution_bitcast_fusion
  267.6 0.0 copy-start.4
  267.6 2.5 collective-permute-start.4
  270.1 35.0 %collective-permute-done.4 = f32[3,64,2048]{2,1,0:T(8,128)S(1)} collective-permute-done((f32[3,64,2048]{2,1,0:T(8,128)S(1)}, f32[3,64,2048]{2,1,0:T(8,128)S(1)}, u32[]{:S(2)}, u32[]{:S(2)}) %collective-permute-start.4) | collective-permute-done | bytes 1572896 | tf_op jit(solution)/shard_map/ppermute | solution.py:56
  305.1 0.2 add.36
  305.3 1.6 collective-permute-start.5
  306.9 34.8 %collective-permute-done.5 = f32[3,64,2048]{2,1,0:T(8,128)S(1)} collective-permute-done((f32[3,64,2048]{2,1,0:T(8,128)S(1)}, f32[3,64,2048]{2,1,0:T(8,128)S(1)}, u32[]{:S(2)}, u32[]{:S(2)}) %collective-permute-start.5) | collective-permute-done | bytes 1572896 | tf_op jit(solution)/shard_map/ppermute | solution.py:56
  341.8 0.2 add.37
  342.0 0.0 copy-start.5
  342.0 2.7 collective-permute-start.6
  344.7 2.8 fusion.13
  347.4 3.1 fusion.6
  350.5 0.0 all-reduce.7.cloned.1.call-update
  350.6 0.0 all-reduce.5.cloned.1.call-start
  350.6 36.4 %all-reduce.7.cloned.1.call-done = (f32[3,512,64]{1,2,0:T(8,128)}, f32[3,512,128]{1,2,0:T(8,128)}) async-done(((f32[3,512,64]{1,2,0:T(8,128)}, f32[3,512,128]{1,2,0:T(8,128)}), (f32[3,512,64]{1,2,0:T(8,128)}, f32[3,512,128]{1,2,0:T(8,128)})) %all-reduce.7.cloned.1.call-update) | async-done | bytes 1179664 | tf_op jit(solution)/shard_map/psum | solution.py:53
  387.0 2.4 convolution_bitcast_fusion.1
  389.4 0.0 all-reduce.5.cloned.1.call-update
  389.4 79.5 %all-reduce.5.cloned.1.call-done = f32[3,128,128]{1,2,0:T(8,128)} async-done(((f32[3,128,128]{1,2,0:T(8,128)}), f32[3,128,128]{1,2,0:T(8,128)}) %all-reduce.5.cloned.1.call-update) | async-done | bytes 196624 | tf_op jit(solution)/shard_map/psum | solution.py:62
  468.9 1.7 copy.32
  470.6 2.7 add.38
  473.4 0.7 copy.37
  (14 shorter events, 0.0 us)
Async XLA Ops:
  7.2 340.3 %copy-start = (bf16[2048,128]{1,0:T(8,128)(2,1)S(1)}, bf16[2048,128]{1,0:T(8,128)(2,1)}, u32[]{:S(2)}) copy-start(bf16[2048,128]{1,0:T(8,128)(2,1)} %param.13) | copy-start | bytes 1572868
  7.2 379.9 %all-reduce.7.cloned.1.call-start = ((), (), s32[]{:S(2)}) async-start(), calls=%async_computation.1 | async-start | bytes 2359296 | tf_op jit(solution)/shard_map/psum | solution.py:53
  10.9 191.4 %collective-permute-start = (bf16[512,127]{0,1:T(8,128)(2,1)}, bf16[512,127]{0,1:T(8,128)(2,1)S(1)}, u32[]{:S(2)}, u32[]{:S(2)}) collective-permute-start(bf16[512,127]{0,1:T(8,128)(2,1)} %get-tuple-element.19), channel_id=1, source_target_pairs={{0,1},{1,2},{2,3},{4,5},{5,6},{6,7},{8,9},{9,10},{10,11},{12,13},{... | collective-permute-start | bytes 390152 | tf_op jit(solution)/shard_map/ppermute | solution.py:12
  13.2 189.1 %collective-permute-start.1 = (bf16[512,127]{0,1:T(8,128)(2,1)}, bf16[512,127]{0,1:T(8,128)(2,1)S(1)}, u32[]{:S(2)}, u32[]{:S(2)}) collective-permute-start(bf16[512,127]{0,1:T(8,128)(2,1)} %get-tuple-element.18), channel_id=1, source_target_pairs={{1,0},{2,1},{3,2},{5,4},{6,5},{7,6},{9,8},{10,9},{11,10},{13,12},{... | collective-permute-start | bytes 390152 | tf_op jit(solution)/shard_map/ppermute | solution.py:15
  223.1 8.0 %copy-start.2 = (bf16[512,16,128]{2,0,1:T(8,128)(2,1)S(1)}, bf16[512,16,128]{2,0,1:T(8,128)(2,1)}, u32[]{:S(2)}) copy-start(bf16[512,16,128]{2,0,1:T(8,128)(2,1)} %copy.27) | copy-start | bytes 6291460
  238.0 20.0 %copy-start.7 = (f32[512]{0:T(512)S(1)}, f32[512]{0:T(512)}, u32[]{:S(2)}) copy-start(f32[512]{0:T(512)} %param.9) | copy-start | bytes 6148
  247.9 5.8 %collective-permute-start.3 = (bf16[3,1,2048]{2,1,0:T(2,128)(2,1)S(1)}, bf16[3,1,2048]{2,1,0:T(2,128)(2,1)S(1)}, u32[]{:S(2)}, u32[]{:S(2)}) collective-permute-start(bf16[3,1,2048]{2,1,0:T(2,128)(2,1)S(1)} %get-tuple-element.15), channel_id=1, source_target_pairs={{0,4},{4,8},{8,12},{12,16},{16,20},{20,24},{24,28},{1,5},{5,9},{9,... | collective-permute-start | bytes 36872 | tf_op jit(solution)/shard_map/ppermute | solution.py:12
  252.2 14.1 %copy-start.6 = (bf16[64,512]{1,0:T(8,128)(2,1)S(1)}, bf16[64,512]{1,0:T(8,128)(2,1)}, u32[]{:S(2)}) copy-start(bf16[64,512]{1,0:T(8,128)(2,1)} %param.11) | copy-start | bytes 196612
  252.2 5.9 %collective-permute-start.2 = (bf16[3,1,2048]{2,1,0:T(2,128)(2,1)S(1)}, bf16[3,1,2048]{2,1,0:T(2,128)(2,1)S(1)}, u32[]{:S(2)}, u32[]{:S(2)}) collective-permute-start(bf16[3,1,2048]{2,1,0:T(2,128)(2,1)S(1)} %get-tuple-element.14), channel_id=1, source_target_pairs={{4,0},{8,4},{12,8},{16,12},{20,16},{24,20},{28,24},{5,1},{9,5},{13... | collective-permute-start | bytes 36872 | tf_op jit(solution)/shard_map/ppermute | solution.py:15
  266.3 81.1 %copy-start.1 = (bf16[3,512,2048]{2,1,0:T(8,128)(2,1)}, bf16[3,512,2048]{2,1,0:T(8,128)(2,1)S(1)}, u32[]{:S(2)}) copy-start(bf16[3,512,2048]{2,1,0:T(8,128)(2,1)S(1)} %multiply_convert_fusion) | copy-start | bytes 18874372
  267.6 77.1 %copy-start.4 = (bf16[2048,64]{0,1:T(8,128)(2,1)S(1)}, bf16[2048,64]{0,1:T(8,128)(2,1)}, u32[]{:S(2)}) copy-start(bf16[2048,64]{0,1:T(8,128)(2,1)} %param.10) | copy-start | bytes 786436
  267.6 37.5 %collective-permute-start.4 = (f32[3,64,2048]{2,1,0:T(8,128)S(1)}, f32[3,64,2048]{2,1,0:T(8,128)S(1)}, u32[]{:S(2)}, u32[]{:S(2)}) collective-permute-start(f32[3,64,2048]{2,1,0:T(8,128)S(1)} %convolution_bitcast_fusion), channel_id=1, source_target_pairs={{0,4},{4,0},{8,12},{12,8},{16,20},{20,16},{24,28},{28,24},{1,5},{5... | collective-permute-start | bytes 4718600 | tf_op jit(solution)/shard_map/ppermute | solution.py:56
  305.3 36.5 %collective-permute-start.5 = (f32[3,64,2048]{2,1,0:T(8,128)S(1)}, f32[3,64,2048]{2,1,0:T(8,128)S(1)}, u32[]{:S(2)}, u32[]{:S(2)}) collective-permute-start(f32[3,64,2048]{2,1,0:T(8,128)S(1)} %add.36), channel_id=1, source_target_pairs={{0,8},{4,12},{8,0},{12,4},{16,24},{20,28},{24,16},{28,20},{1,9},{5... | collective-permute-start | bytes 4718600 | tf_op jit(solution)/shard_map/ppermute | solution.py:56
  342.0 45.0 %copy-start.5 = (bf16[128,512]{1,0:T(8,128)(2,1)S(1)}, bf16[128,512]{1,0:T(8,128)(2,1)}, u32[]{:S(2)}) copy-start(bf16[128,512]{1,0:T(8,128)(2,1)} %param.12) | copy-start | bytes 393220
  342.0 128.6 %collective-permute-start.6 = (f32[3,64,2048]{2,1,0:T(8,128)S(1)}, f32[3,64,2048]{2,1,0:T(8,128)}, u32[]{:S(2)}, u32[]{:S(2)}) collective-permute-start(f32[3,64,2048]{2,1,0:T(8,128)S(1)} %add.37), channel_id=1, source_target_pairs={{0,16},{4,20},{8,24},{12,28},{16,0},{20,4},{24,8},{28,12},{1,17},{... | collective-permute-start | bytes 4718600 | tf_op jit(solution)/shard_map/ppermute | solution.py:56
  350.6 118.3 %all-reduce.5.cloned.1.call-start = ((), (), s32[]{:S(2)}) async-start(), calls=%async_computation | async-start | bytes 393216 | tf_op jit(solution)/shard_map/psum | solution.py:62
  387.0 86.3 %copy-start.3 = (f32[3,512,64]{1,2,0:T(8,128)S(1)}, f32[3,512,64]{1,2,0:T(8,128)}, u32[]{:S(2)}) copy-start(f32[3,512,64]{1,2,0:T(8,128)} %get-tuple-element.23) | copy-start | bytes 1179652
Sparse Core Ops, SparseCore 0:
  350.7 36.2 all-reduce.6
  390.9 77.9 all-reduce.4
